TPU v7x, 512 devices: a whole 4x4x16 slice. The times are simulated.
512 devices in a mesh: docs: 128 (over z_hi, y, x, core), proj: 4 (over z_lo).
Axes of the slice: x: 4, y: 4, z: 16 (z_hi: 4, z_lo: 4; z = z_hi * 4 + z_lo), core: 2. Of those that a mesh axis runs over, the one named last changes fastest.
Arguments:
- grads: bfloat16 [32768, 4096], P('docs', 'proj'), may hold values from -6 to 6
- precond: bfloat16 [4096, 4096], P('docs', 'proj'), may hold values from -3 to 3, as said below
- offsets: int32 [2], replicated, may hold values from 1 to 127
Outputs:
- influence: float32 [2, 32768, 256], P(None, 'docs')
Inputs may be any that keep to these rules, and one draw needn't show every extreme that they name: `precond`: symmetric.
All inputs are finite; a program needn't handle non-finite values.
Results may differ from a plain program's by a relative error of at most 0.014.
Values may be sent and summed in bfloat16 or wider, within the bound.
No kernel may reach another device: no remote copies, remote signals or barrier semaphores. Data moves between devices by JAX's collectives and lax.ppermute only.
A program may use at most 64 MiB of HBM per device.

v0:
```python
import math

import jax
import jax.numpy as jnp
from jax import lax
from jax.sharding import PartitionSpec as P

K = 4096
BOTH = ("docs", "proj")
SPLIT = (17, 19, 21, 23, 25, 27, 29, 31)


def place(index):
    docs, p = divmod(index, 4)
    return docs >> 5, docs >> 3 & 3, docs >> 1 & 3, docs & 1, p


def number(zh, y, x, c, p):
    return ((zh % 4 * 4 + y % 4) * 4 + x % 4) * 8 + c % 2 * 4 + p % 4


def send(value, to):
    return lax.ppermute(value, BOTH, [(i, number(*to(*place(i)))) for i in range(512)])


def put(buffer, piece, at):
    return lax.dynamic_update_slice(
        buffer, piece[None], (at,) + (0,) * (buffer.ndim - 1)
    )


def gather4(value, mine, move):
    out = jnp.zeros((4,) + value.shape, value.dtype)
    out = put(out, value, mine)
    for t in (1, 3, 2):
        out = put(out, send(value, lambda *at: move(t, *at)), (mine - t) % 4)
    return out


def gather_zh(value, mine):
    out = jnp.zeros((4,) + value.shape, value.dtype)
    out = put(out, value, mine)
    for t in (3, 1, 1):
        got = send(value, lambda *at: along_zh(t, *at))
        if t == 1:
            value, mine = got, mine - 1
            out = put(out, got, mine % 4)
        else:
            out = put(out, got, (mine - t) % 4)
    return out


def along_zh(t, zh, y, x, c, p):
    return zh + t, y, x, c, p


def along_first(t, zh, y, x, c, p):
    return zh, y + t * (1 - c), x + t * c, c, p


def along_second(t, zh, y, x, c, p):
    return zh, y + t * c, x + t * (1 - c), c, p


def up_z(zh, y, x, c, p):
    z = 4 * zh + p + 1
    return z // 4, y, x, c, z % 4


def down_z(zh, y, x, c, p):
    z = 4 * zh + p - 1
    return z // 4, y, x, c, z % 4


def rotate(value, by, *more):
    def turn(one, shift):
        def move(zh, y, x, c, p):
            m = (y * 8 + x * 2 + c - shift) % 32
            return zh, m >> 3, m >> 1 & 3, m & 1, p

        return send(one, move) if shift else one

    def branch(shift):
        def run(one, *more):
            if shift in SPLIT:
                one = turn(turn(one, 1), shift - 1)
            else:
                one = turn(one, shift)
            return one, [spread(other) for other in more]

        return run

    return lax.switch(by, [branch(shift) for shift in range(32)], value, *more)


def spread(part):
    return lax.all_to_all(jnp.broadcast_to(part, (4,) + part.shape), "proj", 0, 0)


def total(parts):
    return jnp.sum(parts.astype(jnp.float32), axis=0) * jnp.float32(1.0 / math.sqrt(K))


def on_device(grads, precond, offsets):
    docs, p = lax.axis_index("docs"), lax.axis_index("proj")
    zh, y, x, c = docs >> 5, docs >> 3 & 3, docs >> 1 & 3, docs & 1
    m = docs % 32

    below, above = [grads], [grads]

    def step():
        below.append(send(below[-1], up_z))
        above.append(send(above[-1], down_z))

    def meet(rows):
        rows, below[-1], above[-1] = lax.optimization_barrier(
            (rows, below[-1], above[-1])
        )
        return rows

    step()
    held = meet(gather_zh(precond, (zh - p) % 4))
    step()
    held = meet(gather4(held, jnp.where(c == 0, y, x), along_first))
    step()
    held = gather4(held, jnp.where(c == 0, x, y), along_second)
    step()
    held = meet(held)
    other = send(held, lambda zh, y, x, c, p: (zh, y, x, c ^ 1, p))

    half = grads.shape[0] // 2
    low_half = send(above[4][:half], lambda *at: along_zh(-1, *at))
    high_half = send(below[4][half:], lambda *at: along_zh(1, *at))

    first = jnp.where(c == 0, held, other).transpose(2, 1, 0, 3, 4)
    second = jnp.where(c == 0, other, held).transpose(2, 0, 1, 3, 4)
    rows = jnp.stack([first, second], axis=3).reshape(4, 1024, precond.shape[1])
    slabs = [grads] + [
        jnp.where(p + i < 4, above[i], below[4 - i]) for i in (1, 2, 3)
    ]
    pre = sum(
        jnp.dot(slab, part, preferred_element_type=jnp.float32)
        for slab, part in zip(slabs, rows)
    ).astype(jnp.bfloat16)
    low_half, high_half, pre = lax.optimization_barrier((low_half, high_half, pre))
    blocks = [grads, above[4], jnp.concatenate([low_half, high_half]), below[4]]

    def chosen(offset):
        low = offset % 32
        ahead = (offset // 32 + (m < low)) % 4
        value = blocks[0]
        for i in (1, 2, 3):
            value = jnp.where(ahead == i, blocks[i], value)
        return value, low

    def gram(other):
        return lax.dot_general(
            pre, other, (((1,), (1,)), ((), ())), preferred_element_type=jnp.float32
        ).astype(jnp.bfloat16)

    moved, _ = rotate(*chosen(offsets[0]))
    moved, (ones,) = rotate(*chosen(offsets[1]), gram(moved))
    twos = spread(gram(moved))
    return jnp.stack([total(ones), total(twos)])


def solution(mesh):
    placed = (P("docs", "proj"), P("docs", "proj"), P())
    return jax.shard_map(
        on_device, mesh=mesh, in_specs=placed, out_specs=P(None, "docs", None), check_vma=False
    )
```

profile of v0, /device:TPU:1, one launch (start us, length us, event | category | flops | bytes accessed | tf_op | source)
XLA Modules:
  0.0 214.1 jit_solution(1371875535957218197)
XLA Ops:
  0.0 13.3 %collective-permute-start.78 = (bf16[32,1024]{1,0:T(8,128)(2,1)}, bf16[32,1024]{1,0:T(8,128)(2,1)S(1)}, u32[]{:S(2)}, u32[]{:S(2)}) collective-permute-start(bf16[32,1024]{1,0:T(8,128)(2,1)} %param.68), channel_id=1, source_target_pairs={{0,384},{1,385},{2,386},{3,387},{4,388},{5,389},{6,390},{7,391},{8... | collective-permute-start | bytes 196616 | tf_op jit(solution)/shard_map/ppermute | solution.py:23
  15.2 2.6 %collective-permute-start.81 = (bf16[256,1024]{1,0:T(8,128)(2,1)}, bf16[256,1024]{1,0:T(8,128)(2,1)S(1)}, u32[]{:S(2)}, u32[]{:S(2)}) collective-permute-start(bf16[256,1024]{1,0:T(8,128)(2,1)} %param.67), channel_id=1, source_target_pairs={{0,1},{1,2},{2,3},{3,128},{4,5},{5,6},{6,7},{7,132},{8,9},{9,10},{... | collective-permute-start | bytes 1572872 | tf_op jit(solution)/shard_map/ppermute | solution.py:23
  17.9 5.2 %collective-permute-start.82 = (bf16[256,1024]{1,0:T(8,128)(2,1)}, bf16[256,1024]{1,0:T(8,128)(2,1)S(1)}, u32[]{:S(2)}, u32[]{:S(2)}) collective-permute-start(bf16[256,1024]{1,0:T(8,128)(2,1)} %param.67), channel_id=1, source_target_pairs={{0,387},{1,0},{2,1},{3,2},{4,391},{5,4},{6,5},{7,6},{8,395},{9,8},... | collective-permute-start | bytes 1572872 | tf_op jit(solution)/shard_map/ppermute | solution.py:23
  24.0 3.8 %collective-permute-start.80 = (bf16[32,1024]{1,0:T(8,128)(2,1)S(1)}, bf16[32,1024]{1,0:T(8,128)(2,1)S(1)}, u32[]{:S(2)}, u32[]{:S(2)}) collective-permute-start(bf16[32,1024]{1,0:T(8,128)(2,1)S(1)} %collective-permute-done.79), channel_id=1, source_target_pairs={{0,128},{1,129},{2,130},{3,131},{4,132},{5,133},{6,134},{7,135},{8... | collective-permute-start | bytes 196616 | tf_op jit(solution)/shard_map/ppermute | solution.py:23
  27.9 15.5 %collective-permute-done.80 = bf16[32,1024]{1,0:T(8,128)(2,1)S(1)} collective-permute-done((bf16[32,1024]{1,0:T(8,128)(2,1)S(1)}, bf16[32,1024]{1,0:T(8,128)(2,1)S(1)}, u32[]{:S(2)}, u32[]{:S(2)}) %collective-permute-start.80) | collective-permute-done | bytes 65568 | tf_op jit(solution)/shard_map/ppermute | solution.py:23
  43.4 3.0 %collective-permute-start.83 = (bf16[4,32,1024]{2,1,0:T(8,128)(2,1)S(1)}, bf16[4,32,1024]{2,1,0:T(8,128)(2,1)S(1)}, u32[]{:S(2)}, u32[]{:S(2)}) collective-permute-start(bf16[4,32,1024]{2,1,0:T(8,128)(2,1)S(1)} %bitcast_dynamic-update-slice_fusion.8), channel_id=1, source_target_pairs={{0,32},{1,33},{2,34},{3,35},{4,12},{5,13},{6,14},{7,15},{8,40},{9,... | collective-permute-start | bytes 786440 | tf_op jit(solution)/shard_map/ppermute | solution.py:23
  46.5 3.5 %collective-permute-start.84 = (bf16[4,32,1024]{2,1,0:T(8,128)(2,1)S(1)}, bf16[4,32,1024]{2,1,0:T(8,128)(2,1)S(1)}, u32[]{:S(2)}, u32[]{:S(2)}) collective-permute-start(bf16[4,32,1024]{2,1,0:T(8,128)(2,1)S(1)} %bitcast_dynamic-update-slice_fusion.8), channel_id=1, source_target_pairs={{0,96},{1,97},{2,98},{3,99},{4,28},{5,29},{6,30},{7,31},{8,104},{9... | collective-permute-start | bytes 786440 | tf_op jit(solution)/shard_map/ppermute | solution.py:23
  50.0 3.3 %collective-permute-start.85 = (bf16[4,32,1024]{2,1,0:T(8,128)(2,1)S(1)}, bf16[4,32,1024]{2,1,0:T(8,128)(2,1)S(1)}, u32[]{:S(2)}, u32[]{:S(2)}) collective-permute-start(bf16[4,32,1024]{2,1,0:T(8,128)(2,1)S(1)} %bitcast_dynamic-update-slice_fusion.8), channel_id=1, source_target_pairs={{0,64},{1,65},{2,66},{3,67},{4,20},{5,21},{6,22},{7,23},{8,72},{9,... | collective-permute-start | bytes 786440 | tf_op jit(solution)/shard_map/ppermute | solution.py:23
  55.3 4.6 %collective-permute-start.87 = (bf16[256,1024]{1,0:T(8,128)(2,1)S(1)}, bf16[256,1024]{1,0:T(8,128)(2,1)}, u32[]{:S(2)}, u32[]{:S(2)}) collective-permute-start(bf16[256,1024]{1,0:T(8,128)(2,1)S(1)} %collective-permute-done.82), channel_id=1, source_target_pairs={{0,387},{1,0},{2,1},{3,2},{4,391},{5,4},{6,5},{7,6},{8,395},{9,8},... | collective-permute-start | bytes 1572872 | tf_op jit(solution)/shard_map/ppermute | solution.py:23
  60.1 7.3 %collective-permute-done.86 = bf16[256,1024]{1,0:T(8,128)(2,1)} collective-permute-done((bf16[256,1024]{1,0:T(8,128)(2,1)S(1)}, bf16[256,1024]{1,0:T(8,128)(2,1)}, u32[]{:S(2)}, u32[]{:S(2)}) %collective-permute-start.86) | collective-permute-done | bytes 524320 | tf_op jit(solution)/shard_map/ppermute | solution.py:23
  68.2 4.1 %collective-permute-start.88 = (bf16[4,4,32,1024]{3,2,0,1:T(8,128)(2,1)S(1)}, bf16[4,4,32,1024]{3,2,0,1:T(8,128)(2,1)}, u32[]{:S(2)}, u32[]{:S(2)}) collective-permute-start(bf16[4,4,32,1024]{3,2,0,1:T(8,128)(2,1)S(1)} %bitcast_dynamic-update-slice_fusion.7), channel_id=1, source_target_pairs={{0,8},{1,9},{2,10},{3,11},{4,36},{5,37},{6,38},{7,39},{8,16},{9,17... | collective-permute-start | bytes 3145736 | tf_op jit(solution)/shard_map/ppermute | solution.py:23
  72.3 4.5 %collective-permute-start.89 = (bf16[4,4,32,1024]{3,2,0,1:T(8,128)(2,1)S(1)}, bf16[4,4,32,1024]{3,2,0,1:T(8,128)(2,1)S(1)}, u32[]{:S(2)}, u32[]{:S(2)}) collective-permute-start(bf16[4,4,32,1024]{3,2,0,1:T(8,128)(2,1)S(1)} %bitcast_dynamic-update-slice_fusion.7), channel_id=1, source_target_pairs={{0,24},{1,25},{2,26},{3,27},{4,100},{5,101},{6,102},{7,103},{8,0},... | collective-permute-start | bytes 3145736 | tf_op jit(solution)/shard_map/ppermute | solution.py:23
  76.8 2.9 %collective-permute-start.91 = (bf16[256,1024]{1,0:T(8,128)(2,1)}, bf16[256,1024]{1,0:T(8,128)(2,1)}, u32[]{:S(2)}, u32[]{:S(2)}) collective-permute-start(bf16[256,1024]{1,0:T(8,128)(2,1)} %collective-permute-done.86), channel_id=1, source_target_pairs={{0,1},{1,2},{2,3},{3,128},{4,5},{5,6},{6,7},{7,132},{8,9},{9,10},{... | collective-permute-start | bytes 1572872 | tf_op jit(solution)/shard_map/ppermute | solution.py:23
  79.7 4.4 %collective-permute-start.93 = (bf16[256,1024]{1,0:T(8,128)(2,1)}, bf16[256,1024]{1,0:T(8,128)(2,1)}, u32[]{:S(2)}, u32[]{:S(2)}) collective-permute-start(bf16[256,1024]{1,0:T(8,128)(2,1)} %collective-permute-done.87), channel_id=1, source_target_pairs={{0,387},{1,0},{2,1},{3,2},{4,391},{5,4},{6,5},{7,6},{8,395},{9,8},... | collective-permute-start | bytes 1572872 | tf_op jit(solution)/shard_map/ppermute | solution.py:23
  84.2 3.2 %collective-permute-start.90 = (bf16[4,4,32,1024]{3,2,0,1:T(8,128)(2,1)S(1)}, bf16[4,4,32,1024]{3,2,0,1:T(8,128)(2,1)}, u32[]{:S(2)}, u32[]{:S(2)}) collective-permute-start(bf16[4,4,32,1024]{3,2,0,1:T(8,128)(2,1)S(1)} %bitcast_dynamic-update-slice_fusion.7), channel_id=1, source_target_pairs={{0,16},{1,17},{2,18},{3,19},{4,68},{5,69},{6,70},{7,71},{8,24},{9,... | collective-permute-start | bytes 3145736 | tf_op jit(solution)/shard_map/ppermute | solution.py:23
  87.4 2.6 %broadcast_in_dim.144 = bf16[4,4,4,32,1024]{4,3,1,0,2:T(8,128)(2,1)} broadcast(bf16[]{:T(256)} %constant.149.clone.1), dimensions={} | broadcast | bytes 4194306 | tf_op jit(solution)/shard_map/broadcast_in_dim | solution.py:33
  94.5 4.6 %collective-permute-start.94 = (bf16[256,1024]{1,0:T(8,128)(2,1)}, bf16[256,1024]{1,0:T(8,128)(2,1)S(1)}, u32[]{:S(2)}, u32[]{:S(2)}) collective-permute-start(bf16[256,1024]{1,0:T(8,128)(2,1)} %collective-permute-done.93), channel_id=1, source_target_pairs={{0,387},{1,0},{2,1},{3,2},{4,391},{5,4},{6,5},{7,6},{8,395},{9,8},... | collective-permute-start | bytes 1572872 | tf_op jit(solution)/shard_map/ppermute | solution.py:23
  99.0 2.3 %bitcast_dynamic-update-slice_fusion.1 = bf16[4,4,4,32,1024]{4,3,1,0,2:T(8,128)(2,1)} fusion(bf16[4,4,4,32,1024]{4,3,1,0,2:T(8,128)(2,1)} %bitcast_dynamic-update-slice_fusion.2, s32[]{:T(128)S(6)} %select_n.232, bf16[4,4,32,1024]{3,2,0,1:T(8,128)(2,1)} %collective-permute-done.88), kind=kLoop, calls=%fused_computation.52 | loop fusion | bytes 2097156 | tf_op jit(solution)/shard_map/dynamic_update_slice | solution.py:27
  102.4 2.3 %bitcast_dynamic-update-slice_fusion.3 = bf16[4,4,4,32,1024]{4,3,1,0,2:T(8,128)(2,1)} fusion(bf16[4,4,4,32,1024]{4,3,1,0,2:T(8,128)(2,1)} %bitcast_dynamic-update-slice_fusion, s32[]{:T(128)S(6)} %select_n.236, bf16[4,4,32,1024]{3,2,0,1:T(8,128)(2,1)} %collective-permute-done.90), kind=kLoop, calls=%fused_computation.54 | loop fusion | bytes 2097156 | tf_op jit(solution)/shard_map/dynamic_update_slice | solution.py:27
  107.4 6.0 %collective-permute-start.97 = (bf16[4,4,4,32,1024]{4,3,1,0,2:T(8,128)(2,1)}, bf16[4,4,4,32,1024]{4,3,1,0,2:T(8,128)(2,1)}, u32[]{:S(2)}, u32[]{:S(2)}) collective-permute-start(bf16[4,4,4,32,1024]{4,3,1,0,2:T(8,128)(2,1)} %bitcast_dynamic-update-slice_fusion.3), channel_id=1, source_target_pairs={{0,4},{1,5},{2,6},{3,7},{4,0},{5,1},{6,2},{7,3},{8,12},{9,13},{10,... | collective-permute-start | bytes 12582920 | tf_op jit(solution)/shard_map/ppermute | solution.py:23
  118.9 6.0 %collective-permute-start.95 = (bf16[128,1024]{1,0:T(8,128)(2,1)S(1)}, bf16[128,1024]{1,0:T(8,128)(2,1)S(1)}, u32[]{:S(2)}, u32[]{:S(2)}) collective-permute-start(bf16[128,1024]{1,0:T(8,128)(2,1)S(1)} %slice.17), channel_id=1, source_target_pairs={{0,384},{1,385},{2,386},{3,387},{4,388},{5,389},{6,390},{7,391},{8... | collective-permute-start | bytes 786440 | tf_op jit(solution)/shard_map/ppermute | solution.py:23
  124.9 3.2 %collective-permute-start.96 = (bf16[128,1024]{1,0:T(8,128)(2,1)S(1)}, bf16[128,1024]{1,0:T(8,128)(2,1)S(1)}, u32[]{:S(2)}, u32[]{:S(2)}) collective-permute-start(bf16[128,1024]{1,0:T(8,128)(2,1)S(1)} %slice.18), channel_id=1, source_target_pairs={{0,128},{1,129},{2,130},{3,131},{4,132},{5,133},{6,134},{7,135},{8... | collective-permute-start | bytes 786440 | tf_op jit(solution)/shard_map/ppermute | solution.py:23
  128.2 3.8 %select_bitcast_fusion.1 = (bf16[4,4,4,1,32,1024]{5,4,1,2,0,3:T(8,128)(2,1)S(1)}, bf16[4,4,4,1,32,1024]{5,4,3,2,1,0:T(8,128)(2,1)S(1)}) fusion(bf16[4,4,4,32,1024]{4,3,1,0,2:T(8,128)(2,1)} %bitcast_dynamic-update-slice_fusion.3, bf16[4,4,4,32,1024]{4,3,1,0,2:T(8,128)(2,1)} %collective-permute-done.97, pred[]{:T(512)S(6)} %eq.40), kind=kLoop, calls=%fused_computation.39 | loop fusion | flops 4194304 | bytes 16777216 | tf_op jit(solution)/shard_map/stack | solution.py:137
  139.1 4.4 %collective-permute-done.95 = bf16[128,1024]{1,0:T(8,128)(2,1)S(1)} collective-permute-done((bf16[128,1024]{1,0:T(8,128)(2,1)S(1)}, bf16[128,1024]{1,0:T(8,128)(2,1)S(1)}, u32[]{:S(2)}, u32[]{:S(2)}) %collective-permute-start.95) | collective-permute-done | bytes 262176 | tf_op jit(solution)/shard_map/ppermute | solution.py:23
  145.6 16.3 %conditional.2 = (bf16[256,1024]{1,0:T(8,128)(2,1)S(1)}) conditional(s32[]{:T(128)} %clamp.7, bf16[256,1024]{1,0:T(8,128)(2,1)S(1)} %get-tuple-element.298, bf16[256,1024]{1,0:T(8,128)(2,1)S(1)} %get-tuple-element.298, bf16[256,1024]{1,0:T(8,128)(2,1)S(1)} %get-tuple-element.298, ...), branch_computations={%region_0.1_spmd, %region_1.2_spmd, %region_2.3_spmd, %region_3.4_... | conditional | bytes 5242968 | solution.py:93
  147.5 14.1 %collective-permute-done.10 = bf16[256,1024]{1,0:T(8,128)(2,1)S(1)} collective-permute-done((bf16[256,1024]{1,0:T(8,128)(2,1)S(1)}, bf16[256,1024]{1,0:T(8,128)(2,1)S(1)}, u32[]{:S(2)}, u32[]{:S(2)}) %collective-permute-start.10) | collective-permute-done | bytes 524320 | tf_op jit(solution)/shard_map/cond/branch_11_fun/ppermute | solution.py:23
  162.3 33.4 %conditional.3 = (bf16[256,1024]{1,0:T(8,128)(2,1)}, f32[1,256,256]{2,1,0:T(8,128)S(1)}) conditional(s32[]{:T(128)} %clamp.6, (bf16[256,256]{1,0:T(8,128)(2,1)S(1)}, bf16[256,1024]{1,0:T(8,128)(2,1)}) %tuple.269, (bf16[256,1024]{1,0:T(8,128)(2,1)}, bf16[256,256]{1,0:T(8,128)(2,1)S(1)}) %tuple.270, ...), branch_computations={%region_32.34_spmd, %region_34.36_spmd, %region_36.38_spmd, %regio... | conditional | flops 458752 | bytes 7209088 | solution.py:93
  163.1 13.2 %all-to-all-start.22 = ((bf16[4,256,256]{2,1,0:T(8,128)(2,1)}), bf16[4,256,256]{2,1,0:T(8,128)(2,1)S(1)}, u32[]{:S(2)}, u32[]{:S(2)}) async-start(bf16[4,256,256]{2,1,0:T(8,128)(2,1)} %broadcast_in_dim.118), calls=%async_computation.22 | async-start | bytes 1048576 | tf_op jit(solution)/shard_map/cond/branch_22_fun/all_to_all | solution.py:97
  176.4 3.0 %collective-permute-start.63 = (bf16[256,1024]{1,0:T(8,128)(2,1)}, bf16[256,1024]{1,0:T(8,128)(2,1)S(1)}, u32[]{:S(2)}, u32[]{:S(2)}) collective-permute-start(bf16[256,1024]{1,0:T(8,128)(2,1)} %get-tuple-element.243), channel_id=1, source_target_pairs={{0,40},{1,41},{2,42},{3,43},{4,44},{5,45},{6,46},{7,47},{8,48},{9,... | collective-permute-start | bytes 1572872 | tf_op jit(solution)/shard_map/cond/branch_22_fun/ppermute | solution.py:23
  179.3 15.4 %collective-permute-done.63 = bf16[256,1024]{1,0:T(8,128)(2,1)S(1)} collective-permute-done((bf16[256,1024]{1,0:T(8,128)(2,1)}, bf16[256,1024]{1,0:T(8,128)(2,1)S(1)}, u32[]{:S(2)}, u32[]{:S(2)}) %collective-permute-start.63) | collective-permute-done | bytes 524320 | tf_op jit(solution)/shard_map/cond/branch_22_fun/ppermute | solution.py:23
  197.9 4.3 %all-to-all-start.32 = ((bf16[4,256,256]{2,1,0:T(8,128)(2,1)}), bf16[4,256,256]{2,1,0:T(8,128)(2,1)S(1)}, u32[]{:S(2)}, u32[]{:S(2)}) async-start(bf16[4,256,256]{2,1,0:T(8,128)(2,1)} %broadcast_in_dim.159), calls=%async_computation.32 | async-start | bytes 1048576 | tf_op jit(solution)/shard_map/all_to_all | solution.py:97
  202.1 11.1 %all-to-all-done.32 = bf16[4,256,256]{2,1,0:T(8,128)(2,1)S(1)} async-done(((bf16[4,256,256]{2,1,0:T(8,128)(2,1)}), bf16[4,256,256]{2,1,0:T(8,128)(2,1)S(1)}, u32[]{:S(2)}, u32[]{:S(2)}) %all-to-all-start.32) | async-done | bytes 524320 | tf_op jit(solution)/shard_map/all_to_all | solution.py:97
  (68 shorter events, 30.9 us)
Async XLA Ops:
  0.0 27.8 %collective-permute-start.78 = (bf16[32,1024]{1,0:T(8,128)(2,1)}, bf16[32,1024]{1,0:T(8,128)(2,1)S(1)}, u32[]{:S(2)}, u32[]{:S(2)}) collective-permute-start(bf16[32,1024]{1,0:T(8,128)(2,1)} %param.68), channel_id=1, source_target_pairs={{0,384},{1,385},{2,386},{3,387},{4,388},{5,389},{6,390},{7,391},{8... | collective-permute-start | bytes 196616 | tf_op jit(solution)/shard_map/ppermute | solution.py:23
  13.3 10.7 %collective-permute-start.79 = (bf16[32,1024]{1,0:T(8,128)(2,1)}, bf16[32,1024]{1,0:T(8,128)(2,1)S(1)}, u32[]{:S(2)}, u32[]{:S(2)}) collective-permute-start(bf16[32,1024]{1,0:T(8,128)(2,1)} %param.68), channel_id=1, source_target_pairs={{0,128},{1,129},{2,130},{3,131},{4,132},{5,133},{6,134},{7,135},{8... | collective-permute-start | bytes 196616 | tf_op jit(solution)/shard_map/ppermute | solution.py:23
  15.2 28.1 %collective-permute-start.81 = (bf16[256,1024]{1,0:T(8,128)(2,1)}, bf16[256,1024]{1,0:T(8,128)(2,1)S(1)}, u32[]{:S(2)}, u32[]{:S(2)}) collective-permute-start(bf16[256,1024]{1,0:T(8,128)(2,1)} %param.67), channel_id=1, source_target_pairs={{0,1},{1,2},{2,3},{3,128},{4,5},{5,6},{6,7},{7,132},{8,9},{9,10},{... | collective-permute-start | bytes 1572872 | tf_op jit(solution)/shard_map/ppermute | solution.py:23
  17.9 25.5 %collective-permute-start.82 = (bf16[256,1024]{1,0:T(8,128)(2,1)}, bf16[256,1024]{1,0:T(8,128)(2,1)S(1)}, u32[]{:S(2)}, u32[]{:S(2)}) collective-permute-start(bf16[256,1024]{1,0:T(8,128)(2,1)} %param.67), channel_id=1, source_target_pairs={{0,387},{1,0},{2,1},{3,2},{4,391},{5,4},{6,5},{7,6},{8,395},{9,8},... | collective-permute-start | bytes 1572872 | tf_op jit(solution)/shard_map/ppermute | solution.py:23
  24.0 19.3 %collective-permute-start.80 = (bf16[32,1024]{1,0:T(8,128)(2,1)S(1)}, bf16[32,1024]{1,0:T(8,128)(2,1)S(1)}, u32[]{:S(2)}, u32[]{:S(2)}) collective-permute-start(bf16[32,1024]{1,0:T(8,128)(2,1)S(1)} %collective-permute-done.79), channel_id=1, source_target_pairs={{0,128},{1,129},{2,130},{3,131},{4,132},{5,133},{6,134},{7,135},{8... | collective-permute-start | bytes 196616 | tf_op jit(solution)/shard_map/ppermute | solution.py:23
  43.4 47.7 %copy-start.1 = (bf16[256,1024]{1,0:T(8,128)(2,1)}, bf16[256,1024]{1,0:T(8,128)(2,1)S(1)}, u32[]{:S(2)}) copy-start(bf16[256,1024]{1,0:T(8,128)(2,1)S(1)} %collective-permute-done.81) | copy-start | bytes 1572868
  43.4 24.8 %copy-start.3 = (bf16[256,1024]{1,0:T(8,128)(2,1)}, bf16[256,1024]{1,0:T(8,128)(2,1)S(1)}, u32[]{:S(2)}) copy-start(bf16[256,1024]{1,0:T(8,128)(2,1)S(1)} %collective-permute-done.82) | copy-start | bytes 1572868
  43.4 16.6 %collective-permute-start.83 = (bf16[4,32,1024]{2,1,0:T(8,128)(2,1)S(1)}, bf16[4,32,1024]{2,1,0:T(8,128)(2,1)S(1)}, u32[]{:S(2)}, u32[]{:S(2)}) collective-permute-start(bf16[4,32,1024]{2,1,0:T(8,128)(2,1)S(1)} %bitcast_dynamic-update-slice_fusion.8), channel_id=1, source_target_pairs={{0,32},{1,33},{2,34},{3,35},{4,12},{5,13},{6,14},{7,15},{8,40},{9,... | collective-permute-start | bytes 786440 | tf_op jit(solution)/shard_map/ppermute | solution.py:23
  46.5 13.5 %collective-permute-start.84 = (bf16[4,32,1024]{2,1,0:T(8,128)(2,1)S(1)}, bf16[4,32,1024]{2,1,0:T(8,128)(2,1)S(1)}, u32[]{:S(2)}, u32[]{:S(2)}) collective-permute-start(bf16[4,32,1024]{2,1,0:T(8,128)(2,1)S(1)} %bitcast_dynamic-update-slice_fusion.8), channel_id=1, source_target_pairs={{0,96},{1,97},{2,98},{3,99},{4,28},{5,29},{6,30},{7,31},{8,104},{9... | collective-permute-start | bytes 786440 | tf_op jit(solution)/shard_map/ppermute | solution.py:23
  50.0 10.1 %collective-permute-start.85 = (bf16[4,32,1024]{2,1,0:T(8,128)(2,1)S(1)}, bf16[4,32,1024]{2,1,0:T(8,128)(2,1)S(1)}, u32[]{:S(2)}, u32[]{:S(2)}) collective-permute-start(bf16[4,32,1024]{2,1,0:T(8,128)(2,1)S(1)} %bitcast_dynamic-update-slice_fusion.8), channel_id=1, source_target_pairs={{0,64},{1,65},{2,66},{3,67},{4,20},{5,21},{6,22},{7,23},{8,72},{9,... | collective-permute-start | bytes 786440 | tf_op jit(solution)/shard_map/ppermute | solution.py:23
  53.3 14.1 %collective-permute-start.86 = (bf16[256,1024]{1,0:T(8,128)(2,1)S(1)}, bf16[256,1024]{1,0:T(8,128)(2,1)}, u32[]{:S(2)}, u32[]{:S(2)}) collective-permute-start(bf16[256,1024]{1,0:T(8,128)(2,1)S(1)} %collective-permute-done.81), channel_id=1, source_target_pairs={{0,1},{1,2},{2,3},{3,128},{4,5},{5,6},{6,7},{7,132},{8,9},{9,10},{... | collective-permute-start | bytes 1572872 | tf_op jit(solution)/shard_map/ppermute | solution.py:23
  55.3 13.0 %collective-permute-start.87 = (bf16[256,1024]{1,0:T(8,128)(2,1)S(1)}, bf16[256,1024]{1,0:T(8,128)(2,1)}, u32[]{:S(2)}, u32[]{:S(2)}) collective-permute-start(bf16[256,1024]{1,0:T(8,128)(2,1)S(1)} %collective-permute-done.82), channel_id=1, source_target_pairs={{0,387},{1,0},{2,1},{3,2},{4,391},{5,4},{6,5},{7,6},{8,395},{9,8},... | collective-permute-start | bytes 1572872 | tf_op jit(solution)/shard_map/ppermute | solution.py:23
  68.2 30.8 %collective-permute-start.88 = (bf16[4,4,32,1024]{3,2,0,1:T(8,128)(2,1)S(1)}, bf16[4,4,32,1024]{3,2,0,1:T(8,128)(2,1)}, u32[]{:S(2)}, u32[]{:S(2)}) collective-permute-start(bf16[4,4,32,1024]{3,2,0,1:T(8,128)(2,1)S(1)} %bitcast_dynamic-update-slice_fusion.7), channel_id=1, source_target_pairs={{0,8},{1,9},{2,10},{3,11},{4,36},{5,37},{6,38},{7,39},{8,16},{9,17... | collective-permute-start | bytes 3145736 | tf_op jit(solution)/shard_map/ppermute | solution.py:23
  72.3 29.0 %collective-permute-start.89 = (bf16[4,4,32,1024]{3,2,0,1:T(8,128)(2,1)S(1)}, bf16[4,4,32,1024]{3,2,0,1:T(8,128)(2,1)S(1)}, u32[]{:S(2)}, u32[]{:S(2)}) collective-permute-start(bf16[4,4,32,1024]{3,2,0,1:T(8,128)(2,1)S(1)} %bitcast_dynamic-update-slice_fusion.7), channel_id=1, source_target_pairs={{0,24},{1,25},{2,26},{3,27},{4,100},{5,101},{6,102},{7,103},{8,0},... | collective-permute-start | bytes 3145736 | tf_op jit(solution)/shard_map/ppermute | solution.py:23
  76.8 15.7 %collective-permute-start.91 = (bf16[256,1024]{1,0:T(8,128)(2,1)}, bf16[256,1024]{1,0:T(8,128)(2,1)}, u32[]{:S(2)}, u32[]{:S(2)}) collective-permute-start(bf16[256,1024]{1,0:T(8,128)(2,1)} %collective-permute-done.86), channel_id=1, source_target_pairs={{0,1},{1,2},{2,3},{3,128},{4,5},{5,6},{6,7},{7,132},{8,9},{9,10},{... | collective-permute-start | bytes 1572872 | tf_op jit(solution)/shard_map/ppermute | solution.py:23
  79.7 14.7 %collective-permute-start.93 = (bf16[256,1024]{1,0:T(8,128)(2,1)}, bf16[256,1024]{1,0:T(8,128)(2,1)}, u32[]{:S(2)}, u32[]{:S(2)}) collective-permute-start(bf16[256,1024]{1,0:T(8,128)(2,1)} %collective-permute-done.87), channel_id=1, source_target_pairs={{0,387},{1,0},{2,1},{3,2},{4,391},{5,4},{6,5},{7,6},{8,395},{9,8},... | collective-permute-start | bytes 1572872 | tf_op jit(solution)/shard_map/ppermute | solution.py:23
  84.2 18.3 %collective-permute-start.90 = (bf16[4,4,32,1024]{3,2,0,1:T(8,128)(2,1)S(1)}, bf16[4,4,32,1024]{3,2,0,1:T(8,128)(2,1)}, u32[]{:S(2)}, u32[]{:S(2)}) collective-permute-start(bf16[4,4,32,1024]{3,2,0,1:T(8,128)(2,1)S(1)} %bitcast_dynamic-update-slice_fusion.7), channel_id=1, source_target_pairs={{0,16},{1,17},{2,18},{3,19},{4,68},{5,69},{6,70},{7,71},{8,24},{9,... | collective-permute-start | bytes 3145736 | tf_op jit(solution)/shard_map/ppermute | solution.py:23
  90.0 23.4 %copy-start.5 = (s32[2]{0:T(128)S(1)}, s32[2]{0:T(128)}, u32[]{:S(2)}) copy-start(s32[2]{0:T(128)} %param.69) | copy-start | bytes 28
  92.5 13.8 %collective-permute-start.92 = (bf16[256,1024]{1,0:T(8,128)(2,1)}, bf16[256,1024]{1,0:T(8,128)(2,1)S(1)}, u32[]{:S(2)}, u32[]{:S(2)}) collective-permute-start(bf16[256,1024]{1,0:T(8,128)(2,1)} %collective-permute-done.91), channel_id=1, source_target_pairs={{0,1},{1,2},{2,3},{3,128},{4,5},{5,6},{6,7},{7,132},{8,9},{9,10},{... | collective-permute-start | bytes 1572872 | tf_op jit(solution)/shard_map/ppermute | solution.py:23
  94.5 12.9 %collective-permute-start.94 = (bf16[256,1024]{1,0:T(8,128)(2,1)}, bf16[256,1024]{1,0:T(8,128)(2,1)S(1)}, u32[]{:S(2)}, u32[]{:S(2)}) collective-permute-start(bf16[256,1024]{1,0:T(8,128)(2,1)} %collective-permute-done.93), channel_id=1, source_target_pairs={{0,387},{1,0},{2,1},{3,2},{4,391},{5,4},{6,5},{7,6},{8,395},{9,8},... | collective-permute-start | bytes 1572872 | tf_op jit(solution)/shard_map/ppermute | solution.py:23
  107.4 20.8 %collective-permute-start.97 = (bf16[4,4,4,32,1024]{4,3,1,0,2:T(8,128)(2,1)}, bf16[4,4,4,32,1024]{4,3,1,0,2:T(8,128)(2,1)}, u32[]{:S(2)}, u32[]{:S(2)}) collective-permute-start(bf16[4,4,4,32,1024]{4,3,1,0,2:T(8,128)(2,1)} %bitcast_dynamic-update-slice_fusion.3), channel_id=1, source_target_pairs={{0,4},{1,5},{2,6},{3,7},{4,0},{5,1},{6,2},{7,3},{8,12},{9,13},{10,... | collective-permute-start | bytes 12582920 | tf_op jit(solution)/shard_map/ppermute | solution.py:23
  118.9 24.5 %collective-permute-start.95 = (bf16[128,1024]{1,0:T(8,128)(2,1)S(1)}, bf16[128,1024]{1,0:T(8,128)(2,1)S(1)}, u32[]{:S(2)}, u32[]{:S(2)}) collective-permute-start(bf16[128,1024]{1,0:T(8,128)(2,1)S(1)} %slice.17), channel_id=1, source_target_pairs={{0,384},{1,385},{2,386},{3,387},{4,388},{5,389},{6,390},{7,391},{8... | collective-permute-start | bytes 786440 | tf_op jit(solution)/shard_map/ppermute | solution.py:23
  124.9 19.6 %collective-permute-start.96 = (bf16[128,1024]{1,0:T(8,128)(2,1)S(1)}, bf16[128,1024]{1,0:T(8,128)(2,1)S(1)}, u32[]{:S(2)}, u32[]{:S(2)}) collective-permute-start(bf16[128,1024]{1,0:T(8,128)(2,1)S(1)} %slice.18), channel_id=1, source_target_pairs={{0,128},{1,129},{2,130},{3,131},{4,132},{5,133},{6,134},{7,135},{8... | collective-permute-start | bytes 786440 | tf_op jit(solution)/shard_map/ppermute | solution.py:23
  133.1 2.1 copy-start.4
  133.1 3.1 %copy-start.2 = (bf16[256,1024]{1,0:T(8,128)(2,1)S(1)}, bf16[256,1024]{1,0:T(8,128)(2,1)}, u32[]{:S(2)}) copy-start(bf16[256,1024]{1,0:T(8,128)(2,1)} %copy-done.1) | copy-start | bytes 1572868
  135.2 3.0 %copy-start = (bf16[256,1024]{1,0:T(8,128)(2,1)S(1)}, bf16[256,1024]{1,0:T(8,128)(2,1)}, u32[]{:S(2)}) copy-start(bf16[256,1024]{1,0:T(8,128)(2,1)} %param.67) | copy-start | bytes 1572868
  145.6 16.1 %collective-permute-start.10 = (bf16[256,1024]{1,0:T(8,128)(2,1)S(1)}, bf16[256,1024]{1,0:T(8,128)(2,1)S(1)}, u32[]{:S(2)}, u32[]{:S(2)}) collective-permute-start(bf16[256,1024]{1,0:T(8,128)(2,1)S(1)} %param.11), channel_id=1, source_target_pairs={{0,84},{1,85},{2,86},{3,87},{4,88},{5,89},{6,90},{7,91},{8,92},{9,... | collective-permute-start | bytes 1572872 | tf_op jit(solution)/shard_map/cond/branch_11_fun/ppermute | solution.py:23
  163.1 32.4 %all-to-all-start.22 = ((bf16[4,256,256]{2,1,0:T(8,128)(2,1)}), bf16[4,256,256]{2,1,0:T(8,128)(2,1)S(1)}, u32[]{:S(2)}, u32[]{:S(2)}) async-start(bf16[4,256,256]{2,1,0:T(8,128)(2,1)} %broadcast_in_dim.118), calls=%async_computation.22 | async-start | bytes 1048576 | tf_op jit(solution)/shard_map/cond/branch_22_fun/all_to_all | solution.py:97
  176.4 18.4 %collective-permute-start.63 = (bf16[256,1024]{1,0:T(8,128)(2,1)}, bf16[256,1024]{1,0:T(8,128)(2,1)S(1)}, u32[]{:S(2)}, u32[]{:S(2)}) collective-permute-start(bf16[256,1024]{1,0:T(8,128)(2,1)} %get-tuple-element.243), channel_id=1, source_target_pairs={{0,40},{1,41},{2,42},{3,43},{4,44},{5,45},{6,46},{7,47},{8,48},{9,... | collective-permute-start | bytes 1572872 | tf_op jit(solution)/shard_map/cond/branch_22_fun/ppermute | solution.py:23
  197.9 15.3 %all-to-all-start.32 = ((bf16[4,256,256]{2,1,0:T(8,128)(2,1)}), bf16[4,256,256]{2,1,0:T(8,128)(2,1)S(1)}, u32[]{:S(2)}, u32[]{:S(2)}) async-start(bf16[4,256,256]{2,1,0:T(8,128)(2,1)} %broadcast_in_dim.159), calls=%async_computation.32 | async-start | bytes 1048576 | tf_op jit(solution)/shard_map/all_to_all | solution.py:97
where the time goes:
time: 218 us; the launch traced here: 214 us
  starting transfers between devices  106 us (49%)
  waiting for transfers between devices  73.7 us (34%)
  local copies, waits for them, and re-layouts  13.7 us (6%)
  matrix products  7.63 us (4%)
  other arithmetic  6.88 us (3%)
  between operations  5.58 us (3%)
    ppermute x22, starting transfers between devices, send(): lax.ppermute(value, BOTH, [(i, number(*to(*place(i)))) for i in range(512)])  88.8 us
    ppermute x22, waiting for transfers between devices, send(): lax.ppermute(value, BOTH, [(i, number(*to(*place(i)))) for i in range(512)])  62.7 us
    all_to_all x2, starting transfers between devices, spread(): lax.all_to_all(jnp.broadcast_to(part, (4,) + part.shape), 'proj', 0, 0)  17.5 us
    all_to_all x2, waiting for transfers between devices, spread(): lax.all_to_all(jnp.broadcast_to(part, (4,) + part.shape), 'proj', 0, 0)  11.1 us
    dynamic_update_slice x12, local copies, waits for them, and re-layouts, put(): lax.dynamic_update_slice(buffer, piece[None], (at,) + (0,) * (buffer.ndim...  7.79 us
    dot_general x4, matrix products, on_device(): jnp.dot(slab, part, preferred_element_type=jnp.float32)  5.9 us
    another operation x2, other arithmetic, on_device(): rows = jnp.stack([first, second], axis=3).reshape(4, 1024, precond.shape[1])  4.88 us
  transfers between devices with their start and end apart: 24, of which 11 were waited for; matrix products, arithmetic and copies ran while one was open for 11% of the time, Pallas kernels for 0%

commit v1 on v0

--- a/solution.py
+++ b/solution.py
@@ -7,7 +7,6 @@
 
 K = 4096
 BOTH = ("docs", "proj")
-SPLIT = (17, 19, 21, 23, 25, 27, 29, 31)
 
 
 def place(index):
@@ -29,12 +28,20 @@
     )
 
 
-def gather4(value, mine, move):
-    out = jnp.zeros((4,) + value.shape, value.dtype)
-    out = put(out, value, mine)
-    for t in (1, 3, 2):
-        out = put(out, send(value, lambda *at: move(t, *at)), (mine - t) % 4)
-    return out
+def groups(key):
+    found = {}
+    for docs in range(128):
+        found.setdefault(key(*place(4 * docs)[:4]), []).append(docs)
+    return list(found.values())
+
+
+FIRST = groups(lambda zh, y, x, c: (zh, c, y if c else x))
+SECOND = groups(lambda zh, y, x, c: (zh, c, x if c else y))
+
+
+def spread(part, axis="proj", which=None):
+    parts = jnp.broadcast_to(part, (4,) + part.shape)
+    return lax.all_to_all(parts, axis, 0, 0, axis_index_groups=which)
 
 
 def gather_zh(value, mine):
@@ -54,14 +61,6 @@
     return zh + t, y, x, c, p
 
 
-def along_first(t, zh, y, x, c, p):
-    return zh, y + t * (1 - c), x + t * c, c, p
-
-
-def along_second(t, zh, y, x, c, p):
-    return zh, y + t * c, x + t * (1 - c), c, p
-
-
 def up_z(zh, y, x, c, p):
     z = 4 * zh + p + 1
     return z // 4, y, x, c, z % 4
@@ -72,7 +71,7 @@
     return z // 4, y, x, c, z % 4
 
 
-def rotate(value, by, *more):
+def rotate(value, by):
     def turn(one, shift):
         def move(zh, y, x, c, p):
             m = (y * 8 + x * 2 + c - shift) % 32
@@ -81,30 +80,28 @@
         return send(one, move) if shift else one
 
     def branch(shift):
-        def run(one, *more):
-            if shift in SPLIT:
-                one = turn(turn(one, 1), shift - 1)
-            else:
-                one = turn(one, shift)
-            return one, [spread(other) for other in more]
+        if shift == 31:
+            return lambda one: turn(turn(one, 1), 30)
+        return lambda one: turn(one, shift)
 
-        return run
-
-    return lax.switch(by, [branch(shift) for shift in range(32)], value, *more)
+    return lax.switch(by, [branch(shift) for shift in range(32)], value)
 
 
-def spread(part):
-    return lax.all_to_all(jnp.broadcast_to(part, (4,) + part.shape), "proj", 0, 0)
-
-
-def total(parts):
-    return jnp.sum(parts.astype(jnp.float32), axis=0) * jnp.float32(1.0 / math.sqrt(K))
+def sum_over_proj(part):
+    pieces = part.astype(jnp.bfloat16).reshape((4, -1) + part.shape[-1:])
+    mine = jnp.sum(
+        lax.all_to_all(pieces, "proj", 0, 0).astype(jnp.float32), axis=0
+    ).astype(jnp.bfloat16)
+    return spread(mine).astype(jnp.float32).reshape(part.shape)
 
 
 def on_device(grads, precond, offsets):
     docs, p = lax.axis_index("docs"), lax.axis_index("proj")
-    zh, y, x, c = docs >> 5, docs >> 3 & 3, docs >> 1 & 3, docs & 1
-    m = docs % 32
+    zh, c, m = docs // 32, docs % 2, docs % 32
+    picks = [
+        (offset % 32, (offset // 32 + (m < offset % 32)) % 4)
+        for offset in (offsets[0], offsets[1])
+    ]
 
     below, above = [grads], [grads]
 
@@ -119,11 +116,12 @@
         return rows
 
     step()
+    picks, below[1] = lax.optimization_barrier((picks, below[1]))
     held = meet(gather_zh(precond, (zh - p) % 4))
     step()
-    held = meet(gather4(held, jnp.where(c == 0, y, x), along_first))
+    held = meet(spread(held, "docs", FIRST))
     step()
-    held = gather4(held, jnp.where(c == 0, x, y), along_second)
+    held = spread(held, "docs", SECOND)
     step()
     held = meet(held)
     other = send(held, lambda zh, y, x, c, p: (zh, y, x, c ^ 1, p))
@@ -145,23 +143,22 @@
     low_half, high_half, pre = lax.optimization_barrier((low_half, high_half, pre))
     blocks = [grads, above[4], jnp.concatenate([low_half, high_half]), below[4]]
 
-    def chosen(offset):
-        low = offset % 32
-        ahead = (offset // 32 + (m < low)) % 4
+    def chosen(low, ahead):
         value = blocks[0]
         for i in (1, 2, 3):
             value = jnp.where(ahead == i, blocks[i], value)
         return value, low
 
-    def gram(other):
-        return lax.dot_general(
-            pre, other, (((1,), (1,)), ((), ())), preferred_element_type=jnp.float32
-        ).astype(jnp.bfloat16)
-
-    moved, _ = rotate(*chosen(offsets[0]))
-    moved, (ones,) = rotate(*chosen(offsets[1]), gram(moved))
-    twos = spread(gram(moved))
-    return jnp.stack([total(ones), total(twos)])
+    grams = [
+        lax.dot_general(
+            pre,
+            rotate(*chosen(*where)),
+            (((1,), (1,)), ((), ())),
+            preferred_element_type=jnp.float32,
+        )
+        for where in picks
+    ]
+    return sum_over_proj(jnp.stack(grams)) * jnp.float32(1.0 / math.sqrt(K))
 
 
 def solution(mesh):

time: 218 us -> 241 us (1.11)
  blocking collectives: 0 us -> 24.4 us
  starting transfers between devices: 106 us -> 117 us
  waiting for transfers between devices: 73.7 us -> 67.5 us
  matrix products: 7.63 us -> 4.39 us
    all_to_all x0 -> x2, blocking collectives: none -> 24.4 us  [the longest x1 15.8 us: sum_over_proj(): lax.all_to_all(pieces, 'proj', 0, 0).astype(jnp.float32)]
    all_to_all x2, waiting for transfers between devices: 11.1 us -> 0.01 us  [spread(): return lax.all_to_all(parts, axis, 0, 0, axis_index_groups=which)]
    ppermute x22 -> x16, starting transfers between devices: 88.8 us -> 96.4 us  [send(): lax.ppermute(value, BOTH, [(i, number(*to(*place(i)))) for i in range(512)])]
    dynamic_update_slice x12 -> x4, local copies, waits for them, and re-layouts: 7.79 us -> 0.88 us  [put(): lax.dynamic_update_slice(buffer, piece[None], (at,) + (0,) * (buffer.ndim...]
    optimization_barrier x0 -> x2, local copies, waits for them, and re-layouts: none -> 5.19 us  [meet(): lax.optimization_barrier((rows, below[-1], above[-1]))]
    ppermute x22 -> x16, waiting for transfers between devices: 62.7 us -> 67.5 us  [send(): lax.ppermute(value, BOTH, [(i, number(*to(*place(i)))) for i in range(512)])]
    all_to_all x2, starting transfers between devices: 17.5 us -> 20.6 us  [spread(): return lax.all_to_all(parts, axis, 0, 0, axis_index_groups=which)]
  transfers between devices with their start and end apart: 24 -> 18, of which waited for: 11 -> 9; matrix products, arithmetic and copies ran while one was open for 11% -> 5% of each run, Pallas kernels for 0% -> 0%
where the time goes in v1:
time: 241 us; the launch traced here: 237 us
  starting transfers between devices  117 us (49%)
  waiting for transfers between devices  67.5 us (28%)
  blocking collectives  24.4 us (10%)
  local copies, waits for them, and re-layouts  11.4 us (5%)
  other arithmetic  5.97 us (2%)
  between operations  5.71 us (2%)
  matrix products  4.39 us (2%)
    ppermute x16, starting transfers between devices, send(): lax.ppermute(value, BOTH, [(i, number(*to(*place(i)))) for i in range(512)])  96.4 us
    ppermute x16, waiting for transfers between devices, send(): lax.ppermute(value, BOTH, [(i, number(*to(*place(i)))) for i in range(512)])  67.5 us
    all_to_all x2, starting transfers between devices, spread(): return lax.all_to_all(parts, axis, 0, 0, axis_index_groups=which)  20.6 us
    all_to_all x1, blocking collectives, sum_over_proj(): lax.all_to_all(pieces, 'proj', 0, 0).astype(jnp.float32)  15.8 us
    all_to_all x1, blocking collectives, spread(): return lax.all_to_all(parts, axis, 0, 0, axis_index_groups=which)  8.58 us
    optimization_barrier x2, local copies, waits for them, and re-layouts, meet(): lax.optimization_barrier((rows, below[-1], above[-1]))  5.19 us
    another operation x2, other arithmetic, on_device(): rows = jnp.stack([first, second], axis=3).reshape(4, 1024, precond.shape[1])  4.89 us
  transfers between devices with their start and end apart: 18, of which 9 were waited for; matrix products, arithmetic and copies ran while one was open for 5% of the time, Pallas kernels for 0%

profile of v1, /device:TPU:1, one launch (start us, length us, event | category | flops | bytes accessed | tf_op | source)
XLA Modules:
  0.0 236.9 jit_solution(16122889913270908145)
XLA Ops:
  0.0 13.3 %collective-permute-start.64 = (bf16[32,1024]{1,0:T(8,128)(2,1)}, bf16[32,1024]{1,0:T(8,128)(2,1)S(1)}, u32[]{:S(2)}, u32[]{:S(2)}) collective-permute-start(bf16[32,1024]{1,0:T(8,128)(2,1)} %param.68), channel_id=1, source_target_pairs={{0,384},{1,385},{2,386},{3,387},{4,388},{5,389},{6,390},{7,391},{8... | collective-permute-start | bytes 196616 | tf_op jit(solution)/shard_map/ppermute | solution.py:22
  13.3 1.9 collective-permute-start.65
  15.2 2.6 %collective-permute-start.67 = (bf16[256,1024]{1,0:T(8,128)(2,1)}, bf16[256,1024]{1,0:T(8,128)(2,1)S(1)}, u32[]{:S(2)}, u32[]{:S(2)}) collective-permute-start(bf16[256,1024]{1,0:T(8,128)(2,1)} %param.67), channel_id=1, source_target_pairs={{0,1},{1,2},{2,3},{3,128},{4,5},{5,6},{6,7},{7,132},{8,9},{9,10},{... | collective-permute-start | bytes 1572872 | tf_op jit(solution)/shard_map/ppermute | solution.py:22
  17.9 5.2 %collective-permute-start.68 = (bf16[256,1024]{1,0:T(8,128)(2,1)}, bf16[256,1024]{1,0:T(8,128)(2,1)S(1)}, u32[]{:S(2)}, u32[]{:S(2)}) collective-permute-start(bf16[256,1024]{1,0:T(8,128)(2,1)} %param.67), channel_id=1, source_target_pairs={{0,387},{1,0},{2,1},{3,2},{4,391},{5,4},{6,5},{7,6},{8,395},{9,8},... | collective-permute-start | bytes 1572872 | tf_op jit(solution)/shard_map/ppermute | solution.py:22
  30.6 3.8 %collective-permute-start.66 = (bf16[32,1024]{1,0:T(8,128)(2,1)S(1)}, bf16[32,1024]{1,0:T(8,128)(2,1)S(1)}, u32[]{:S(2)}, u32[]{:S(2)}) collective-permute-start(bf16[32,1024]{1,0:T(8,128)(2,1)S(1)} %collective-permute-done.65), channel_id=1, source_target_pairs={{0,128},{1,129},{2,130},{3,131},{4,132},{5,133},{6,134},{7,135},{8... | collective-permute-start | bytes 196616 | tf_op jit(solution)/shard_map/ppermute | solution.py:22
  34.4 5.8 %collective-permute-done.66 = bf16[32,1024]{1,0:T(8,128)(2,1)S(1)} collective-permute-done((bf16[32,1024]{1,0:T(8,128)(2,1)S(1)}, bf16[32,1024]{1,0:T(8,128)(2,1)S(1)}, u32[]{:S(2)}, u32[]{:S(2)}) %collective-permute-start.66) | collective-permute-done | bytes 65568 | tf_op jit(solution)/shard_map/ppermute | solution.py:22
  41.4 15.8 %all-to-all-start = ((bf16[4,4,32,1024]{3,2,1,0:T(8,128)(2,1)}), bf16[4,4,32,1024]{3,2,1,0:T(8,128)(2,1)S(1)}, u32[]{:S(2)}, u32[]{:S(2)}) async-start(bf16[4,4,32,1024]{3,2,1,0:T(8,128)(2,1)} %broadcast_in_dim.29), calls=%async_computation | async-start | bytes 2097152 | tf_op jit(solution)/shard_map/all_to_all | solution.py:44
  57.2 3.4 %collective-permute-start.69 = (bf16[256,1024]{1,0:T(8,128)(2,1)S(1)}, bf16[256,1024]{1,0:T(8,128)(2,1)S(1)}, u32[]{:S(2)}, u32[]{:S(2)}) collective-permute-start(bf16[256,1024]{1,0:T(8,128)(2,1)S(1)} %collective-permute-done.67), channel_id=1, source_target_pairs={{0,1},{1,2},{2,3},{3,128},{4,5},{5,6},{6,7},{7,132},{8,9},{9,10},{... | collective-permute-start | bytes 1572872 | tf_op jit(solution)/shard_map/ppermute | solution.py:22
  60.6 6.9 %collective-permute-start.70 = (bf16[256,1024]{1,0:T(8,128)(2,1)S(1)}, bf16[256,1024]{1,0:T(8,128)(2,1)S(1)}, u32[]{:S(2)}, u32[]{:S(2)}) collective-permute-start(bf16[256,1024]{1,0:T(8,128)(2,1)S(1)} %collective-permute-done.68), channel_id=1, source_target_pairs={{0,387},{1,0},{2,1},{3,2},{4,391},{5,4},{6,5},{7,6},{8,395},{9,8},... | collective-permute-start | bytes 1572872 | tf_op jit(solution)/shard_map/ppermute | solution.py:22
  67.5 9.7 %collective-permute-done.69 = bf16[256,1024]{1,0:T(8,128)(2,1)S(1)} collective-permute-done((bf16[256,1024]{1,0:T(8,128)(2,1)S(1)}, bf16[256,1024]{1,0:T(8,128)(2,1)S(1)}, u32[]{:S(2)}, u32[]{:S(2)}) %collective-permute-start.69) | collective-permute-done | bytes 524320 | tf_op jit(solution)/shard_map/ppermute | solution.py:22
  78.2 2.7 %broadcast_in_dim.30 = bf16[4,4,4,32,1024]{4,3,1,2,0:T(8,128)(2,1)} broadcast(bf16[4,4,32,1024]{3,2,0,1:T(8,128)(2,1)S(1)} %copy.15), dimensions={1,2,3,4} | broadcast | bytes 5242880 | tf_op jit(solution)/shard_map/broadcast_in_dim | solution.py:43
  80.9 4.8 %all-to-all-start.1 = ((bf16[4,4,4,32,1024]{4,3,1,2,0:T(8,128)(2,1)}), bf16[4,4,4,32,1024]{4,3,1,2,0:T(8,128)(2,1)}, u32[]{:S(2)}, u32[]{:S(2)}) async-start(bf16[4,4,4,32,1024]{4,3,1,2,0:T(8,128)(2,1)} %broadcast_in_dim.30), calls=%async_computation.1 | async-start | bytes 8388608 | tf_op jit(solution)/shard_map/all_to_all | solution.py:44
  85.7 1.9 collective-permute-start.71
  87.6 5.3 %collective-permute-start.73 = (bf16[256,1024]{1,0:T(8,128)(2,1)S(1)}, bf16[256,1024]{1,0:T(8,128)(2,1)S(1)}, u32[]{:S(2)}, u32[]{:S(2)}) collective-permute-start(bf16[256,1024]{1,0:T(8,128)(2,1)S(1)} %collective-permute-done.70), channel_id=1, source_target_pairs={{0,387},{1,0},{2,1},{3,2},{4,391},{5,4},{6,5},{7,6},{8,395},{9,8},... | collective-permute-start | bytes 1572872 | tf_op jit(solution)/shard_map/ppermute | solution.py:22
  93.0 8.9 %collective-permute-done.71 = bf16[256,1024]{1,0:T(8,128)(2,1)S(1)} collective-permute-done((bf16[256,1024]{1,0:T(8,128)(2,1)S(1)}, bf16[256,1024]{1,0:T(8,128)(2,1)S(1)}, u32[]{:S(2)}, u32[]{:S(2)}) %collective-permute-start.71) | collective-permute-done | bytes 524320 | tf_op jit(solution)/shard_map/ppermute | solution.py:22
  101.8 1.9 collective-permute-start.72
  103.8 4.6 %collective-permute-start.74 = (bf16[256,1024]{1,0:T(8,128)(2,1)S(1)}, bf16[256,1024]{1,0:T(8,128)(2,1)S(1)}, u32[]{:S(2)}, u32[]{:S(2)}) collective-permute-start(bf16[256,1024]{1,0:T(8,128)(2,1)S(1)} %collective-permute-done.73), channel_id=1, source_target_pairs={{0,387},{1,0},{2,1},{3,2},{4,391},{5,4},{6,5},{7,6},{8,395},{9,8},... | collective-permute-start | bytes 1572872 | tf_op jit(solution)/shard_map/ppermute | solution.py:22
  108.3 7.9 %collective-permute-done.72 = bf16[256,1024]{1,0:T(8,128)(2,1)S(1)} collective-permute-done((bf16[256,1024]{1,0:T(8,128)(2,1)S(1)}, bf16[256,1024]{1,0:T(8,128)(2,1)S(1)}, u32[]{:S(2)}, u32[]{:S(2)}) %collective-permute-start.72) | collective-permute-done | bytes 524320 | tf_op jit(solution)/shard_map/ppermute | solution.py:22
  117.2 5.1 %copy.17 = bf16[4,4,4,32,1024]{4,3,1,0,2:T(8,128)(2,1)} copy(bf16[4,4,4,32,1024]{4,3,1,2,0:T(8,128)(2,1)} %all-to-all-done.1) | data formatting | bytes 8388608 | tf_op jit(solution)/shard_map/optimization_barrier | solution.py:113
  122.3 18.7 %collective-permute-start.77 = (bf16[4,4,4,32,1024]{4,3,1,0,2:T(8,128)(2,1)}, bf16[4,4,4,32,1024]{4,3,1,0,2:T(8,128)(2,1)}, u32[]{:S(2)}, u32[]{:S(2)}) collective-permute-start(bf16[4,4,4,32,1024]{4,3,1,0,2:T(8,128)(2,1)} %copy.17), channel_id=1, source_target_pairs={{0,4},{1,5},{2,6},{3,7},{4,0},{5,1},{6,2},{7,3},{8,12},{9,13},{10,... | collective-permute-start | bytes 12582920 | tf_op jit(solution)/shard_map/ppermute | solution.py:22
  141.1 10.3 %collective-permute-start.75 = (bf16[128,1024]{1,0:T(8,128)(2,1)S(1)}, bf16[128,1024]{1,0:T(8,128)(2,1)S(1)}, u32[]{:S(2)}, u32[]{:S(2)}) collective-permute-start(bf16[128,1024]{1,0:T(8,128)(2,1)S(1)} %slice.18), channel_id=1, source_target_pairs={{0,384},{1,385},{2,386},{3,387},{4,388},{5,389},{6,390},{7,391},{8... | collective-permute-start | bytes 786440 | tf_op jit(solution)/shard_map/ppermute | solution.py:22
  151.4 1.9 collective-permute-start.76
  153.4 3.8 %select_bitcast_fusion.1 = (bf16[4,4,4,1,32,1024]{5,4,1,2,0,3:T(8,128)(2,1)S(1)}, bf16[4,4,4,1,32,1024]{5,4,3,2,1,0:T(8,128)(2,1)S(1)}) fusion(bf16[4,4,4,32,1024]{4,3,1,0,2:T(8,128)(2,1)} %collective-permute-done.77, pred[]{:T(512)S(6)} %eq.35, bf16[4,4,4,32,1024]{4,3,1,2,0:T(8,128)(2,1)} %all-to-all-done.1), kind=kLoop, calls=%fused_computation.7 | loop fusion | flops 4194304 | bytes 16777216 | tf_op jit(solution)/shard_map/stack | solution.py:135
  162.1 11.8 %collective-permute-done.75 = bf16[128,1024]{1,0:T(8,128)(2,1)S(1)} collective-permute-done((bf16[128,1024]{1,0:T(8,128)(2,1)S(1)}, bf16[128,1024]{1,0:T(8,128)(2,1)S(1)}, u32[]{:S(2)}, u32[]{:S(2)}) %collective-permute-start.75) | collective-permute-done | bytes 262176 | tf_op jit(solution)/shard_map/ppermute | solution.py:22
  174.1 16.0 %conditional.2 = (bf16[256,1024]{1,0:T(8,128)(2,1)S(1)}) conditional(s32[]{:T(128)} %clamp.6, bf16[256,1024]{1,0:T(8,128)(2,1)S(1)} %get-tuple-element.175, bf16[256,1024]{1,0:T(8,128)(2,1)S(1)} %get-tuple-element.175, bf16[256,1024]{1,0:T(8,128)(2,1)S(1)} %get-tuple-element.175, ...), branch_computations={%region_0.1_spmd, %region_1.2_spmd, %region_2.3_spmd, %region_3.4_... | conditional | bytes 5242968 | solution.py:87
  174.2 5.4 %collective-permute-start.5 = (bf16[256,1024]{1,0:T(8,128)(2,1)S(1)}, bf16[256,1024]{1,0:T(8,128)(2,1)S(1)}, u32[]{:S(2)}, u32[]{:S(2)}) collective-permute-start(bf16[256,1024]{1,0:T(8,128)(2,1)S(1)} %param.6), channel_id=1, source_target_pairs={{0,104},{1,105},{2,106},{3,107},{4,108},{5,109},{6,110},{7,111},{8... | collective-permute-start | bytes 1572872 | tf_op jit(solution)/shard_map/cond/branch_6_fun/ppermute | solution.py:22
  179.6 10.3 %collective-permute-done.5 = bf16[256,1024]{1,0:T(8,128)(2,1)S(1)} collective-permute-done((bf16[256,1024]{1,0:T(8,128)(2,1)S(1)}, bf16[256,1024]{1,0:T(8,128)(2,1)S(1)}, u32[]{:S(2)}, u32[]{:S(2)}) %collective-permute-start.5) | collective-permute-done | bytes 524320 | tf_op jit(solution)/shard_map/cond/branch_6_fun/ppermute | solution.py:22
  190.5 20.6 %conditional.3 = (bf16[256,1024]{1,0:T(8,128)(2,1)S(1)}) conditional(s32[]{:T(128)} %clamp.7, bf16[256,1024]{1,0:T(8,128)(2,1)S(1)} %get-tuple-element.176, bf16[256,1024]{1,0:T(8,128)(2,1)S(1)} %get-tuple-element.176, bf16[256,1024]{1,0:T(8,128)(2,1)S(1)} %get-tuple-element.176, ...), branch_computations={%region_32.33_spmd, %region_33.34_spmd, %region_34.35_spmd, %regio... | conditional | bytes 5242968 | solution.py:87
  190.6 9.2 %collective-permute-start.34 = (bf16[256,1024]{1,0:T(8,128)(2,1)S(1)}, bf16[256,1024]{1,0:T(8,128)(2,1)S(1)}, u32[]{:S(2)}, u32[]{:S(2)}) collective-permute-start(bf16[256,1024]{1,0:T(8,128)(2,1)S(1)} %param.35), channel_id=1, source_target_pairs={{0,116},{1,117},{2,118},{3,119},{4,120},{5,121},{6,122},{7,123},{8... | collective-permute-start | bytes 1572872 | tf_op jit(solution)/shard_map/cond/branch_3_fun/ppermute | solution.py:22
  199.7 11.3 %collective-permute-done.34 = bf16[256,1024]{1,0:T(8,128)(2,1)S(1)} collective-permute-done((bf16[256,1024]{1,0:T(8,128)(2,1)S(1)}, bf16[256,1024]{1,0:T(8,128)(2,1)S(1)}, u32[]{:S(2)}, u32[]{:S(2)}) %collective-permute-start.34) | collective-permute-done | bytes 524320 | tf_op jit(solution)/shard_map/cond/branch_3_fun/ppermute | solution.py:22
  211.5 15.8 %all_to_all.20 = bf16[4,128,256]{2,1,0:T(8,128)(2,1)S(1)} all-to-all(bf16[4,128,256]{2,1,0:T(8,128)(2,1)S(1)} %bitcast.51), channel_id=1, replica_groups=mesh['docs'=128,'proj'=4] {'proj'}, dimensions={0} | all-to-all | bytes 524288 | tf_op jit(solution)/shard_map/all_to_all | solution.py:93
  227.4 8.6 %all_to_all.21 = bf16[4,128,256]{2,1,0:T(8,128)(2,1)S(1)} all-to-all(bf16[4,128,256]{2,1,0:T(8,128)(2,1)S(1)} %broadcast_in_dim.31), channel_id=1, replica_groups=mesh['docs'=128,'proj'=4] {'proj'}, dimensions={0} | all-to-all | bytes 524288 | tf_op jit(solution)/shard_map/all_to_all | solution.py:44
  (47 shorter events, 12.0 us)
Async XLA Ops:
  0.0 34.4 %collective-permute-start.64 = (bf16[32,1024]{1,0:T(8,128)(2,1)}, bf16[32,1024]{1,0:T(8,128)(2,1)S(1)}, u32[]{:S(2)}, u32[]{:S(2)}) collective-permute-start(bf16[32,1024]{1,0:T(8,128)(2,1)} %param.68), channel_id=1, source_target_pairs={{0,384},{1,385},{2,386},{3,387},{4,388},{5,389},{6,390},{7,391},{8... | collective-permute-start | bytes 196616 | tf_op jit(solution)/shard_map/ppermute | solution.py:22
  13.3 17.3 %collective-permute-start.65 = (bf16[32,1024]{1,0:T(8,128)(2,1)}, bf16[32,1024]{1,0:T(8,128)(2,1)S(1)}, u32[]{:S(2)}, u32[]{:S(2)}) collective-permute-start(bf16[32,1024]{1,0:T(8,128)(2,1)} %param.68), channel_id=1, source_target_pairs={{0,128},{1,129},{2,130},{3,131},{4,132},{5,133},{6,134},{7,135},{8... | collective-permute-start | bytes 196616 | tf_op jit(solution)/shard_map/ppermute | solution.py:22
  15.2 25.0 %collective-permute-start.67 = (bf16[256,1024]{1,0:T(8,128)(2,1)}, bf16[256,1024]{1,0:T(8,128)(2,1)S(1)}, u32[]{:S(2)}, u32[]{:S(2)}) collective-permute-start(bf16[256,1024]{1,0:T(8,128)(2,1)} %param.67), channel_id=1, source_target_pairs={{0,1},{1,2},{2,3},{3,128},{4,5},{5,6},{6,7},{7,132},{8,9},{9,10},{... | collective-permute-start | bytes 1572872 | tf_op jit(solution)/shard_map/ppermute | solution.py:22
  17.9 22.4 %collective-permute-start.68 = (bf16[256,1024]{1,0:T(8,128)(2,1)}, bf16[256,1024]{1,0:T(8,128)(2,1)S(1)}, u32[]{:S(2)}, u32[]{:S(2)}) collective-permute-start(bf16[256,1024]{1,0:T(8,128)(2,1)} %param.67), channel_id=1, source_target_pairs={{0,387},{1,0},{2,1},{3,2},{4,391},{5,4},{6,5},{7,6},{8,395},{9,8},... | collective-permute-start | bytes 1572872 | tf_op jit(solution)/shard_map/ppermute | solution.py:22
  30.6 9.7 %collective-permute-start.66 = (bf16[32,1024]{1,0:T(8,128)(2,1)S(1)}, bf16[32,1024]{1,0:T(8,128)(2,1)S(1)}, u32[]{:S(2)}, u32[]{:S(2)}) collective-permute-start(bf16[32,1024]{1,0:T(8,128)(2,1)S(1)} %collective-permute-done.65), channel_id=1, source_target_pairs={{0,128},{1,129},{2,130},{3,131},{4,132},{5,133},{6,134},{7,135},{8... | collective-permute-start | bytes 196616 | tf_op jit(solution)/shard_map/ppermute | solution.py:22
  41.4 36.7 %all-to-all-start = ((bf16[4,4,32,1024]{3,2,1,0:T(8,128)(2,1)}), bf16[4,4,32,1024]{3,2,1,0:T(8,128)(2,1)S(1)}, u32[]{:S(2)}, u32[]{:S(2)}) async-start(bf16[4,4,32,1024]{3,2,1,0:T(8,128)(2,1)} %broadcast_in_dim.29), calls=%async_computation | async-start | bytes 2097152 | tf_op jit(solution)/shard_map/all_to_all | solution.py:44
  57.2 20.0 %collective-permute-start.69 = (bf16[256,1024]{1,0:T(8,128)(2,1)S(1)}, bf16[256,1024]{1,0:T(8,128)(2,1)S(1)}, u32[]{:S(2)}, u32[]{:S(2)}) collective-permute-start(bf16[256,1024]{1,0:T(8,128)(2,1)S(1)} %collective-permute-done.67), channel_id=1, source_target_pairs={{0,1},{1,2},{2,3},{3,128},{4,5},{5,6},{6,7},{7,132},{8,9},{9,10},{... | collective-permute-start | bytes 1572872 | tf_op jit(solution)/shard_map/ppermute | solution.py:22
  60.6 17.5 %collective-permute-start.70 = (bf16[256,1024]{1,0:T(8,128)(2,1)S(1)}, bf16[256,1024]{1,0:T(8,128)(2,1)S(1)}, u32[]{:S(2)}, u32[]{:S(2)}) collective-permute-start(bf16[256,1024]{1,0:T(8,128)(2,1)S(1)} %collective-permute-done.68), channel_id=1, source_target_pairs={{0,387},{1,0},{2,1},{3,2},{4,391},{5,4},{6,5},{7,6},{8,395},{9,8},... | collective-permute-start | bytes 1572872 | tf_op jit(solution)/shard_map/ppermute | solution.py:22
  77.2 8.5 %copy-start.1 = (bf16[256,1024]{1,0:T(8,128)(2,1)}, bf16[256,1024]{1,0:T(8,128)(2,1)S(1)}, u32[]{:S(2)}) copy-start(bf16[256,1024]{1,0:T(8,128)(2,1)S(1)} %collective-permute-done.69) | copy-start | bytes 1572868
  78.1 9.6 %copy-start.3 = (bf16[256,1024]{1,0:T(8,128)(2,1)}, bf16[256,1024]{1,0:T(8,128)(2,1)S(1)}, u32[]{:S(2)}) copy-start(bf16[256,1024]{1,0:T(8,128)(2,1)S(1)} %collective-permute-done.70) | copy-start | bytes 1572868
  80.9 36.3 %all-to-all-start.1 = ((bf16[4,4,4,32,1024]{4,3,1,2,0:T(8,128)(2,1)}), bf16[4,4,4,32,1024]{4,3,1,2,0:T(8,128)(2,1)}, u32[]{:S(2)}, u32[]{:S(2)}) async-start(bf16[4,4,4,32,1024]{4,3,1,2,0:T(8,128)(2,1)} %broadcast_in_dim.30), calls=%async_computation.1 | async-start | bytes 8388608 | tf_op jit(solution)/shard_map/all_to_all | solution.py:44
  85.7 16.1 %collective-permute-start.71 = (bf16[256,1024]{1,0:T(8,128)(2,1)S(1)}, bf16[256,1024]{1,0:T(8,128)(2,1)S(1)}, u32[]{:S(2)}, u32[]{:S(2)}) collective-permute-start(bf16[256,1024]{1,0:T(8,128)(2,1)S(1)} %collective-permute-done.69), channel_id=1, source_target_pairs={{0,1},{1,2},{2,3},{3,128},{4,5},{5,6},{6,7},{7,132},{8,9},{9,10},{... | collective-permute-start | bytes 1572872 | tf_op jit(solution)/shard_map/ppermute | solution.py:22
  87.6 16.1 %collective-permute-start.73 = (bf16[256,1024]{1,0:T(8,128)(2,1)S(1)}, bf16[256,1024]{1,0:T(8,128)(2,1)S(1)}, u32[]{:S(2)}, u32[]{:S(2)}) collective-permute-start(bf16[256,1024]{1,0:T(8,128)(2,1)S(1)} %collective-permute-done.70), channel_id=1, source_target_pairs={{0,387},{1,0},{2,1},{3,2},{4,391},{5,4},{6,5},{7,6},{8,395},{9,8},... | collective-permute-start | bytes 1572872 | tf_op jit(solution)/shard_map/ppermute | solution.py:22
  101.8 14.4 %collective-permute-start.72 = (bf16[256,1024]{1,0:T(8,128)(2,1)S(1)}, bf16[256,1024]{1,0:T(8,128)(2,1)S(1)}, u32[]{:S(2)}, u32[]{:S(2)}) collective-permute-start(bf16[256,1024]{1,0:T(8,128)(2,1)S(1)} %collective-permute-done.71), channel_id=1, source_target_pairs={{0,1},{1,2},{2,3},{3,128},{4,5},{5,6},{6,7},{7,132},{8,9},{9,10},{... | collective-permute-start | bytes 1572872 | tf_op jit(solution)/shard_map/ppermute | solution.py:22
  103.8 13.4 %collective-permute-start.74 = (bf16[256,1024]{1,0:T(8,128)(2,1)S(1)}, bf16[256,1024]{1,0:T(8,128)(2,1)S(1)}, u32[]{:S(2)}, u32[]{:S(2)}) collective-permute-start(bf16[256,1024]{1,0:T(8,128)(2,1)S(1)} %collective-permute-done.73), channel_id=1, source_target_pairs={{0,387},{1,0},{2,1},{3,2},{4,391},{5,4},{6,5},{7,6},{8,395},{9,8},... | collective-permute-start | bytes 1572872 | tf_op jit(solution)/shard_map/ppermute | solution.py:22
  122.3 31.1 %collective-permute-start.77 = (bf16[4,4,4,32,1024]{4,3,1,0,2:T(8,128)(2,1)}, bf16[4,4,4,32,1024]{4,3,1,0,2:T(8,128)(2,1)}, u32[]{:S(2)}, u32[]{:S(2)}) collective-permute-start(bf16[4,4,4,32,1024]{4,3,1,0,2:T(8,128)(2,1)} %copy.17), channel_id=1, source_target_pairs={{0,4},{1,5},{2,6},{3,7},{4,0},{5,1},{6,2},{7,3},{8,12},{9,13},{10,... | collective-permute-start | bytes 12582920 | tf_op jit(solution)/shard_map/ppermute | solution.py:22
  141.1 32.8 %collective-permute-start.75 = (bf16[128,1024]{1,0:T(8,128)(2,1)S(1)}, bf16[128,1024]{1,0:T(8,128)(2,1)S(1)}, u32[]{:S(2)}, u32[]{:S(2)}) collective-permute-start(bf16[128,1024]{1,0:T(8,128)(2,1)S(1)} %slice.18), channel_id=1, source_target_pairs={{0,384},{1,385},{2,386},{3,387},{4,388},{5,389},{6,390},{7,391},{8... | collective-permute-start | bytes 786440 | tf_op jit(solution)/shard_map/ppermute | solution.py:22
  151.4 22.5 %collective-permute-start.76 = (bf16[128,1024]{1,0:T(8,128)(2,1)S(1)}, bf16[128,1024]{1,0:T(8,128)(2,1)S(1)}, u32[]{:S(2)}, u32[]{:S(2)}) collective-permute-start(bf16[128,1024]{1,0:T(8,128)(2,1)S(1)} %slice.19), channel_id=1, source_target_pairs={{0,128},{1,129},{2,130},{3,131},{4,132},{5,133},{6,134},{7,135},{8... | collective-permute-start | bytes 786440 | tf_op jit(solution)/shard_map/ppermute | solution.py:22
  157.2 1.1 copy-start.2
  157.2 1.2 copy-start.4
  159.3 2.0 copy-start
  174.2 15.7 %collective-permute-start.5 = (bf16[256,1024]{1,0:T(8,128)(2,1)S(1)}, bf16[256,1024]{1,0:T(8,128)(2,1)S(1)}, u32[]{:S(2)}, u32[]{:S(2)}) collective-permute-start(bf16[256,1024]{1,0:T(8,128)(2,1)S(1)} %param.6), channel_id=1, source_target_pairs={{0,104},{1,105},{2,106},{3,107},{4,108},{5,109},{6,110},{7,111},{8... | collective-permute-start | bytes 1572872 | tf_op jit(solution)/shard_map/cond/branch_6_fun/ppermute | solution.py:22
  190.6 20.5 %collective-permute-start.34 = (bf16[256,1024]{1,0:T(8,128)(2,1)S(1)}, bf16[256,1024]{1,0:T(8,128)(2,1)S(1)}, u32[]{:S(2)}, u32[]{:S(2)}) collective-permute-start(bf16[256,1024]{1,0:T(8,128)(2,1)S(1)} %param.35), channel_id=1, source_target_pairs={{0,116},{1,117},{2,118},{3,119},{4,120},{5,121},{6,122},{7,123},{8... | collective-permute-start | bytes 1572872 | tf_op jit(solution)/shard_map/cond/branch_3_fun/ppermute | solution.py:22
